TPU v7x, 512 devices: a whole 4x4x16 slice. The times are simulated.
512 devices in a mesh: face: 4 (over z_lo), tile: 64 (over y, z_hi, x), lev: 2 (over core).
Axes of the slice: x: 4, y: 4, z: 16 (z_hi: 4, z_lo: 4; z = z_hi * 4 + z_lo), core: 2. Of those that a mesh axis runs over, the one named last changes fastest.
Arguments:
- flux: float32 [2048, 8, 512], P(('face', 'tile')), may hold values from -6 to 6
- profile: float32 [16], P('lev'), may hold values from 0.2 to 1
- courant: float32 [2, 16, 512, 2048], P(None, 'lev', 'tile', 'face'), may hold values from 0.05 to 0.45
- winds: int32 [2, 16, 512, 2048], P(None, 'lev', 'tile', 'face'), may hold values from 0 to 1
- cells: int32 [64, 4, 128], P('tile', 'face'), may hold values from 0 to 4095, as said below
- counts: int32 [64, 4], P('tile', 'face'), may hold values from 32 to 128, as said below
- kernels: float32 [16, 64, 4, 128], P('lev', 'tile', 'face'), may hold values from 0.25 to 0.75
- month_weight: float32 [8, 64, 4, 128], P(None, 'tile', 'face'), may hold values from 0 to 1
- observed: float32 [64, 4, 128], P('tile', 'face'), may hold values from -8 to 8
- obs_weight: float32 [64, 4, 128], P('tile', 'face'), may hold values from 0.5 to 2
- precision: float32 [8], replicated, may hold values from 0.5 to 2
Outputs:
- flux_gradient: float32 [8, 512, 2048], P(None, 'tile', 'face')
- precision_gradient: float32 [8], replicated
Inputs may be any that keep to these rules, and one draw needn't show every extreme that they name: Within each block the 128 entries are distinct cells, numbered row by row over the block's 8 rows of 512 cells; the first four slots of every block hold, in some order, a cell of the block's first column, one of its last column, and interior cells of its first row and of its last row. `counts`: slot s of a block holds a sounding when s is below the block's count; some block is full and some holds exactly 32.
All inputs are finite; a program needn't handle non-finite values.
Results may differ from a plain program's by a relative error of at most 0.00015.
Values sent between devices are 32-bit elements; how exact they have to be, the bound alone decides.
A program may use at most 64 MiB of HBM per device.

v0:
```python
import jax
import jax.numpy as jnp
from jax import lax
from jax.sharding import PartitionSpec as P

KAPPA = 0.025


def extended(x, sides, width, wrap):
    for axis, dim in sides:
        devices, length = (lax.axis_size(axis), x.shape[dim])
        up = [(i, (i + 1) % devices) for i in range(devices if wrap else devices - 1)]
        down = [(j, i) for i, j in up]
        last = lax.slice_in_dim(x, length - width, length, axis=dim)
        initial = lax.slice_in_dim(x, 0, width, axis=dim)
        before = lax.ppermute(last, axis, up)
        after = lax.ppermute(initial, axis, down)
        x = jnp.concatenate([before, x, after], axis=dim)
    return x


def shifted(x, axis, by):
    devices = lax.axis_size(axis)
    return lax.ppermute(x, axis, [(i, (i + by) % devices) for i in range(devices)])


def shifted_2(value, axis, steps):
    count = lax.axis_size(axis)
    initial, last = (max(0, -steps), min(count, count - steps))
    return lax.ppermute(value, axis, [(source, source + steps) for source in range(initial, last)])


def weights_from(speed_x, speed_y, east_flag, north_flag):
    w_west = speed_x * (1.0 - east_flag) + KAPPA
    w_east = speed_x * east_flag + KAPPA
    w_south = speed_y * (1.0 - north_flag) + KAPPA
    w_north = speed_y * north_flag + KAPPA
    w_centre = 1.0 - speed_x - speed_y - 4.0 * KAPPA
    return (w_centre, w_west, w_east, w_south, w_north)


def flags_of(winds):
    return ((winds[0] == 1).astype(jnp.float32), (winds[1] == 1).astype(jnp.float32))


def advance(conc, coeffs):
    w_centre, w_west, w_east, w_south, w_north = coeffs
    side = extended(conc, (("face", 3),), 1, True)
    rim = extended(conc, (("tile", 2),), 1, False)
    return (
        w_centre * conc
        + w_west * side[..., :-2]
        + w_east * side[..., 2:]
        + w_south * rim[..., :-2, :]
        + w_north * rim[..., 2:, :]
    )


def retreat(grad, coeffs):
    w_centre, w_west, w_east, w_south, w_north = coeffs
    west_weighted = w_west * grad
    east_weighted = w_east * grad
    south_weighted = w_south * grad
    north_weighted = w_north * grad
    from_east = shifted(west_weighted[..., :1], "face", -1)
    from_west = shifted(east_weighted[..., -1:], "face", 1)
    from_above = shifted_2(south_weighted[..., :1, :], "tile", -1)
    from_below = shifted_2(north_weighted[..., -1:, :], "tile", 1)
    west_part = jnp.concatenate([west_weighted[..., 1:], from_east], -1)
    east_part = jnp.concatenate([from_west, east_weighted[..., :-1]], -1)
    south_part = jnp.concatenate([south_weighted[..., 1:, :], from_above], -2)
    north_part = jnp.concatenate([from_below, north_weighted[..., :-1, :]], -2)
    return w_centre * grad + west_part + east_part + south_part + north_part


def on_device(
    flux,
    profile,
    courant,
    winds,
    cells,
    counts,
    kernels,
    month_weight,
    observed,
    obs_weight,
    precision,
):
    n_tracer = flux.shape[1]
    n_level = profile.shape[0]
    slot_total = cells.shape[2]
    moved = lax.all_to_all(flux, "tile", split_axis=2, concat_axis=0, tiled=True)
    field = jnp.transpose(moved, (1, 2, 0))
    rows_dev = field.shape[1]
    cols_dev = field.shape[2]
    n_cell = rows_dev * cols_dev
    east_flag, north_flag = flags_of(winds)
    conc = profile[None, :, None, None] * field[:, None]
    coeffs = weights_from(courant[0], courant[1], east_flag, north_flag)
    conc = advance(advance(conc, coeffs), coeffs)
    slot_cells = cells.reshape(slot_total)
    live = jnp.arange(slot_total, dtype=jnp.int32) < counts.reshape(())
    picker = jnp.where(
        live[:, None] & (slot_cells[:, None] == jnp.arange(n_cell, dtype=jnp.int32)[None, :]),
        1.0,
        0.0,
    ).astype(jnp.float32)
    flat = conc.reshape(n_tracer, n_level, n_cell)
    sampled = jnp.einsum("tlc,sc->tls", flat, picker, precision=lax.Precision.HIGHEST)
    kern = kernels.reshape(n_level, slot_total)
    monthly = month_weight.reshape(n_tracer, slot_total)
    partial_model = jnp.sum(kern * jnp.sum(monthly[:, None, :] * sampled, 0), 0)
    model = lax.psum(partial_model, "lev")
    forcing = jnp.where(
        live, obs_weight.reshape(slot_total) * (observed.reshape(slot_total) - model), 0.0
    )
    values = kern[None] * (monthly * forcing[None])[:, None, :]
    lam = jnp.einsum("tls,sc->tlc", values, picker, precision=lax.Precision.HIGHEST)
    lam = lam.reshape(n_tracer, n_level, rows_dev, cols_dev)
    lam = retreat(retreat(lam, coeffs), coeffs)
    adj_part = jnp.sum(profile[None, :, None, None] * lam, 1)
    all_cells = n_cell * lax.axis_size("tile") * lax.axis_size("face")
    adj = lax.psum(adj_part, "lev")
    flux_gradient = precision[:, None, None] * field - adj
    square_sum = lax.psum(jnp.sum(adj * adj, axis=(1, 2)), ("face", "tile"))
    precision_gradient = 0.5 / precision - 0.5 * (square_sum / all_cells) / (precision * precision)
    return (flux_gradient, precision_gradient)


def solution(mesh):
    return jax.shard_map(
        on_device,
        mesh=mesh,
        in_specs=(
            P(("face", "tile"), None, None),
            P("lev"),
            P(None, "lev", "tile", "face"),
            P(None, "lev", "tile", "face"),
            P("tile", "face", None),
            P("tile", "face"),
            P("lev", "tile", "face", None),
            P(None, "tile", "face", None),
            P("tile", "face", None),
            P("tile", "face", None),
            P(),
        ),
        out_specs=(P(None, "tile", "face"), P()),
        check_vma=False,
    )
```

profile of v0, /device:TPU:32, one launch (start us, length us, event | category | flops | bytes accessed | tf_op | source)
XLA Modules:
  0.0 1168.7 jit_solution(5610475102505204907)
XLA Ops:
  7.2 1.7 copy.25
  8.9 1.7 reshape.69
  10.6 20.3 %all-to-all-start = ((f32[64,1,512]{2,1,0:T(1,128)}), f32[64,1,512]{2,1,0:T(1,128)S(1)}, u32[]{:S(2)}, u32[]{:S(2)}) async-start(f32[64,1,512]{2,1,0:T(1,128)} %reshape.69), calls=%async_computation | async-start | bytes 262144 | tf_op jit(solution)/shard_map/all_to_all | solution.py:92
  31.1 20.0 %all-to-all-done = f32[64,1,512]{2,1,0:T(1,128)S(1)} async-done(((f32[64,1,512]{2,1,0:T(1,128)}), f32[64,1,512]{2,1,0:T(1,128)S(1)}, u32[]{:S(2)}, u32[]{:S(2)}) %all-to-all-start) | async-done | bytes 131104 | tf_op jit(solution)/shard_map/all_to_all | solution.py:92
  53.7 2.4 copy.27
  56.1 2.8 all_to_all.16
  59.3 2.5 collective-permute-start.2
  61.8 1.3 collective-permute-start.3
  63.1 2.9 collective-permute-start
  66.1 2.9 collective-permute-start.1
  70.1 4.1 collective-permute-done
  74.2 7.7 collective-permute-done.1
  82.7 1.3 collective-permute-start.6
  85.5 5.5 collective-permute-start.4
  91.0 1.9 collective-permute-start.5
  93.0 7.6 collective-permute-done.4
  101.3 2.4 fusion.12
  103.8 2.6 psum.21
  106.5 1.7 fusion
  110.1 4.9 collective-permute-start.11
  115.2 3.2 collective-permute-start.8
  118.4 3.1 collective-permute-start.9
  122.2 3.8 collective-permute-done.8
  126.0 6.6 collective-permute-done.9
  133.6 4.2 collective-permute-start.12
  138.6 5.9 collective-permute-start.15
  146.0 3.7 collective-permute-start.13
  149.8 7.5 collective-permute-done.13
  157.8 9.1 collective-permute-done.14
  168.8 66.5 %all-reduce.2.cloned.1.call-done = f32[8,8,512]{2,1,0:T(8,128)} async-done(((f32[8,8,512]{2,1,0:T(8,128)}), f32[8,8,512]{2,1,0:T(8,128)}) %all-reduce.2.cloned.1.call-update) | async-done | bytes 131088 | tf_op jit(solution)/shard_map/psum | solution.py:123
  235.3 1.7 multiply_reduce_fusion.1
  237.0 924.4 %psum.23 = f32[8]{0:T(128)S(1)} all-reduce(f32[8]{0:T(128)S(1)} %get-tuple-element.33), channel_id=1, replica_groups=mesh['face'=4,'tile'=64,'lev'=2] {'face','tile'}, use_global_device_ids=true, to_apply=%region_6.7 | all-reduce | flops 8 | bytes 64 | tf_op jit(solution)/shard_map/psum | solution.py:125
  (78 shorter events, 15.5 us)
Async XLA Ops:
  7.2 23.8 %copy-start = (f32[2,8,8,512]{3,2,1,0:T(8,128)S(1)}, f32[2,8,8,512]{3,2,1,0:T(8,128)}, u32[]{:S(2)}) copy-start(f32[2,8,8,512]{3,2,1,0:T(8,128)} %param.13) | copy-start | bytes 786436
  7.2 23.8 %copy-start.1 = (s32[2,8,8,512]{3,2,1,0:T(8,128)S(1)}, s32[2,8,8,512]{3,2,1,0:T(8,128)}, u32[]{:S(2)}) copy-start(s32[2,8,8,512]{3,2,1,0:T(8,128)} %param.14) | copy-start | bytes 786436
  10.6 40.5 %all-to-all-start = ((f32[64,1,512]{2,1,0:T(1,128)}), f32[64,1,512]{2,1,0:T(1,128)S(1)}, u32[]{:S(2)}, u32[]{:S(2)}) async-start(f32[64,1,512]{2,1,0:T(1,128)} %reshape.69), calls=%async_computation | async-start | bytes 262144 | tf_op jit(solution)/shard_map/all_to_all | solution.py:92
  30.9 204.3 %all-reduce.2.cloned.1.call-start = ((), (), s32[]{:S(2)}) async-start(), calls=%async_computation.1 | async-start | bytes 262144 | tf_op jit(solution)/shard_map/psum | solution.py:123
  56.1 2.8 copy-start.4
  59.3 22.6 %collective-permute-start.2 = (f32[8,8,1,512]{3,1,2,0:T(8,128)S(1)}, f32[8,8,1,512]{3,1,2,0:T(8,128)S(1)}, u32[]{:S(2)}, u32[]{:S(2)}) collective-permute-start(f32[8,8,1,512]{3,1,2,0:T(8,128)S(1)} %get-tuple-element.25), channel_id=1, source_target_pairs={{0,2},{2,4},{4,6},{6,8},{8,10},{10,12},{12,14},{14,16},{16,18},{18... | collective-permute-start | bytes 393224 | tf_op jit(solution)/shard_map/ppermute | solution.py:16
  61.8 20.1 %collective-permute-start.3 = (f32[8,8,1,512]{3,1,2,0:T(8,128)S(1)}, f32[8,8,1,512]{3,1,2,0:T(8,128)S(1)}, u32[]{:S(2)}, u32[]{:S(2)}) collective-permute-start(f32[8,8,1,512]{3,1,2,0:T(8,128)S(1)} %get-tuple-element.26), channel_id=1, source_target_pairs={{2,0},{4,2},{6,4},{8,6},{10,8},{12,10},{14,12},{16,14},{18,16},{20... | collective-permute-start | bytes 393224 | tf_op jit(solution)/shard_map/ppermute | solution.py:17
  63.1 11.1 collective-permute-start
  66.1 15.9 %collective-permute-start.1 = (f32[8,8,8,1]{3,1,2,0:T(8,128)S(1)}, f32[8,8,8,1]{3,1,2,0:T(8,128)S(1)}, u32[]{:S(2)}, u32[]{:S(2)}) collective-permute-start(f32[8,8,8,1]{3,1,2,0:T(8,128)S(1)} %get-tuple-element.24), channel_id=1, source_target_pairs={{128,0},{256,128},{384,256},{0,384},{129,1},{257,129},{385,257},{1... | collective-permute-start | bytes 6152 | tf_op jit(solution)/shard_map/ppermute | solution.py:17
  82.7 17.8 %collective-permute-start.6 = (f32[8,8,1,512]{3,1,2,0:T(8,128)S(1)}, f32[8,8,1,512]{3,1,2,0:T(8,128)S(1)}, u32[]{:S(2)}, u32[]{:S(2)}) collective-permute-start(f32[8,8,1,512]{3,1,2,0:T(8,128)S(1)} %get-tuple-element.21), channel_id=1, source_target_pairs={{0,2},{2,4},{4,6},{6,8},{8,10},{10,12},{12,14},{14,16},{16,18},{18... | collective-permute-start | bytes 393224 | tf_op jit(solution)/shard_map/ppermute | solution.py:16
  84.0 17.3 %copy-start.2 = (f32[8,1,1,128]{3,2,1,0:T(1,128)S(1)}, f32[8,1,1,128]{3,2,1,0:T(1,128)}, u32[]{:S(2)}) copy-start(f32[8,1,1,128]{3,2,1,0:T(1,128)} %param.18) | copy-start | bytes 12292
  84.0 17.3 %copy-start.8 = (s32[1,1,128]{2,1,0:T(1,128)S(1)}, s32[1,1,128]{2,1,0:T(1,128)}, u32[]{:S(2)}) copy-start(s32[1,1,128]{2,1,0:T(1,128)} %param.15) | copy-start | bytes 1540
  84.0 16.5 %collective-permute-start.7 = (f32[8,8,1,512]{3,1,2,0:T(8,128)S(1)}, f32[8,8,1,512]{3,1,2,0:T(8,128)S(1)}, u32[]{:S(2)}, u32[]{:S(2)}) collective-permute-start(f32[8,8,1,512]{3,1,2,0:T(8,128)S(1)} %get-tuple-element.22), channel_id=1, source_target_pairs={{2,0},{4,2},{6,4},{8,6},{10,8},{12,10},{14,12},{16,14},{18,16},{20... | collective-permute-start | bytes 393224 | tf_op jit(solution)/shard_map/ppermute | solution.py:17
  85.5 15.0 %collective-permute-start.4 = (f32[8,8,8,1]{3,1,2,0:T(8,128)S(1)}, f32[8,8,8,1]{3,1,2,0:T(8,128)S(1)}, u32[]{:S(2)}, u32[]{:S(2)}) collective-permute-start(f32[8,8,8,1]{3,1,2,0:T(8,128)S(1)} %get-tuple-element.19), channel_id=1, source_target_pairs={{0,128},{128,256},{256,384},{384,0},{1,129},{129,257},{257,385},{3... | collective-permute-start | bytes 6152 | tf_op jit(solution)/shard_map/ppermute | solution.py:16
  91.0 9.6 collective-permute-start.5
  92.9 10.9 copy-start.3
  92.9 13.5 %copy-start.6 = (f32[1,1,128]{2,1,0:T(1,128)S(1)}, f32[1,1,128]{2,1,0:T(1,128)}, u32[]{:S(2)}) copy-start(f32[1,1,128]{2,1,0:T(1,128)} %param.19) | copy-start | bytes 1540
  92.9 13.5 %copy-start.7 = (f32[1,1,128]{2,1,0:T(1,128)S(1)}, f32[1,1,128]{2,1,0:T(1,128)}, u32[]{:S(2)}) copy-start(f32[1,1,128]{2,1,0:T(1,128)} %param.20) | copy-start | bytes 1540
  108.8 23.7 %collective-permute-start.10 = (f32[8,8,1,512]{3,1,2,0:T(8,128)S(1)}, f32[8,8,1,512]{3,1,2,0:T(8,128)S(1)}, u32[]{:S(2)}, u32[]{:S(2)}) collective-permute-start(f32[8,8,1,512]{3,1,2,0:T(8,128)S(1)} %slice.165), channel_id=1, source_target_pairs={{2,0},{4,2},{6,4},{8,6},{10,8},{12,10},{14,12},{16,14},{18,16},{20... | collective-permute-start | bytes 393224 | tf_op jit(solution)/shard_map/ppermute | solution.py:30
  110.1 22.4 %collective-permute-start.11 = (f32[8,8,1,512]{3,1,2,0:T(8,128)S(1)}, f32[8,8,1,512]{3,1,2,0:T(8,128)S(1)}, u32[]{:S(2)}, u32[]{:S(2)}) collective-permute-start(f32[8,8,1,512]{3,1,2,0:T(8,128)S(1)} %slice.166), channel_id=1, source_target_pairs={{0,2},{2,4},{4,6},{6,8},{8,10},{10,12},{12,14},{14,16},{16,18},{18... | collective-permute-start | bytes 393224 | tf_op jit(solution)/shard_map/ppermute | solution.py:30
  115.2 10.7 collective-permute-start.8
  118.4 14.1 %collective-permute-start.9 = (f32[8,8,8,1]{3,1,2,0:T(8,128)S(1)}, f32[8,8,8,1]{3,1,2,0:T(8,128)S(1)}, u32[]{:S(2)}, u32[]{:S(2)}) collective-permute-start(f32[8,8,8,1]{3,1,2,0:T(8,128)S(1)} %slice.162), channel_id=1, source_target_pairs={{0,128},{128,256},{256,384},{384,0},{1,129},{129,257},{257,385},{3... | collective-permute-start | bytes 6152 | tf_op jit(solution)/shard_map/ppermute | solution.py:24
  133.6 16.0 %collective-permute-start.12 = (f32[8,8,8,1]{3,1,2,0:T(8,128)S(1)}, f32[8,8,8,1]{3,1,2,0:T(8,128)S(1)}, u32[]{:S(2)}, u32[]{:S(2)}) collective-permute-start(f32[8,8,8,1]{3,1,2,0:T(8,128)S(1)} %slice.169), channel_id=1, source_target_pairs={{0,384},{128,0},{256,128},{384,256},{1,385},{129,1},{257,129},{385... | collective-permute-start | bytes 6152 | tf_op jit(solution)/shard_map/ppermute | solution.py:24
  138.6 19.1 %collective-permute-start.15 = (f32[8,8,1,512]{3,1,2,0:T(8,128)S(1)}, f32[8,8,1,512]{3,1,2,0:T(8,128)S(1)}, u32[]{:S(2)}, u32[]{:S(2)}) collective-permute-start(f32[8,8,1,512]{3,1,2,0:T(8,128)S(1)} %slice.174), channel_id=1, source_target_pairs={{0,2},{2,4},{4,6},{6,8},{8,10},{10,12},{12,14},{14,16},{16,18},{18... | collective-permute-start | bytes 393224 | tf_op jit(solution)/shard_map/ppermute | solution.py:30
  144.5 22.3 %collective-permute-start.14 = (f32[8,8,1,512]{3,1,2,0:T(8,128)S(1)}, f32[8,8,1,512]{3,1,2,0:T(8,128)S(1)}, u32[]{:S(2)}, u32[]{:S(2)}) collective-permute-start(f32[8,8,1,512]{3,1,2,0:T(8,128)S(1)} %slice.173), channel_id=1, source_target_pairs={{2,0},{4,2},{6,4},{8,6},{10,8},{12,10},{14,12},{16,14},{18,16},{20... | collective-permute-start | bytes 393224 | tf_op jit(solution)/shard_map/ppermute | solution.py:30
  146.0 11.4 collective-permute-start.13
  166.9 68.3 %copy-start.5 = (f32[8]{0:T(128)S(1)}, f32[8]{0:T(128)}, u32[]{:S(2)}) copy-start(f32[8]{0:T(128)} %param.21) | copy-start | bytes 100
Sparse Core Ops, SparseCore 0:
  169.0 66.2 all-reduce.1
where the time goes:
time: 1170 us
  blocking collectives  927 us (79%)
  waiting for transfers between devices  133 us (11%)
  starting transfers between devices  67.6 us (6%)
  between operations  15.2 us (1%)
  local copies, waits for them, and re-layouts  13.2 us (1%)
    psum x1, blocking collectives, on_device(): square_sum = lax.psum(jnp.sum(adj * adj, axis=(1, 2)), ('face', 'tile'))  924 us
    psum x1, waiting for transfers between devices, on_device(): adj = lax.psum(adj_part, 'lev')  66.5 us
  transfers between devices with their start and end apart: 18, of which 9 were waited for; matrix products, arithmetic and copies ran while one was open for 0% of the time, Pallas kernels for 0%

commit v1 on v0

--- a/solution.py
+++ b/solution.py
@@ -122,7 +122,7 @@
     all_cells = n_cell * lax.axis_size("tile") * lax.axis_size("face")
     adj = lax.psum(adj_part, "lev")
     flux_gradient = precision[:, None, None] * field - adj
-    square_sum = lax.psum(jnp.sum(adj * adj, axis=(1, 2)), ("face", "tile"))
+    square_sum = lax.psum(lax.psum(jnp.sum(adj * adj, axis=(1, 2)), "face"), "tile")
     precision_gradient = 0.5 / precision - 0.5 * (square_sum / all_cells) / (precision * precision)
     return (flux_gradient, precision_gradient)
 

time: 1170 us -> 480 us (0.41)
  blocking collectives: 927 us -> 237 us
    psum x1 -> x2, blocking collectives: 924 us -> 235 us  [the longest x1 225 us: on_device(): lax.psum(lax.psum(jnp.sum(adj * adj, axis=(1, 2)), 'face'), 'tile')]
  transfers between devices with their start and end apart: 18 -> 18, of which waited for: 9 -> 9; matrix products, arithmetic and copies ran while one was open for 0% -> 1% of each run, Pallas kernels for 0% -> 0%
where the time goes in v1:
time: 480 us; the launch traced here: 479 us
  blocking collectives  237 us (49%)
  waiting for transfers between devices  133 us (28%)
  starting transfers between devices  67.6 us (14%)
  between operations  15.2 us (3%)
  local copies, waits for them, and re-layouts  13.2 us (3%)
  other arithmetic  8.64 us (2%)
    psum x1, blocking collectives, on_device(): lax.psum(lax.psum(jnp.sum(adj * adj, axis=(1, 2)), 'face'), 'tile')  225 us
    psum x1, waiting for transfers between devices, on_device(): adj = lax.psum(adj_part, 'lev')  66.4 us
    all_to_all x1, starting transfers between devices, on_device(): lax.all_to_all(flux, 'tile', split_axis=2, concat_axis=0, tiled=True)  20.3 us
    all_to_all x1, waiting for transfers between devices, on_device(): lax.all_to_all(flux, 'tile', split_axis=2, concat_axis=0, tiled=True)  20 us
    ppermute x4, waiting for transfers between devices, shifted(): lax.ppermute(x, axis, [(i, (i + by) % devices) for i in range(devices)])  17.9 us
    ppermute x4, starting transfers between devices, shifted(): lax.ppermute(x, axis, [(i, (i + by) % devices) for i in range(devices)])  14.3 us
    ppermute x4, starting transfers between devices, shifted_2(): lax.ppermute(value, axis, [(source, source + steps) for source in range(i...  13.4 us
    ppermute x4, starting transfers between devices, extended(): before = lax.ppermute(last, axis, up)  12.2 us
  transfers between devices with their start and end apart: 18, of which 9 were waited for; matrix products, arithmetic and copies ran while one was open for 1% of the time, Pallas kernels for 0%

profile of v1, /device:TPU:32, one launch (start us, length us, event | category | flops | bytes accessed | tf_op | source)
XLA Modules:
  0.0 478.9 jit_solution(14641408444181761715)
XLA Ops:
  7.2 1.7 copy.25
  8.9 1.7 reshape.69
  10.6 20.3 %all-to-all-start = ((f32[64,1,512]{2,1,0:T(1,128)}), f32[64,1,512]{2,1,0:T(1,128)S(1)}, u32[]{:S(2)}, u32[]{:S(2)}) async-start(f32[64,1,512]{2,1,0:T(1,128)} %reshape.69), calls=%async_computation | async-start | bytes 262144 | tf_op jit(solution)/shard_map/all_to_all | solution.py:92
  31.1 20.0 %all-to-all-done = f32[64,1,512]{2,1,0:T(1,128)S(1)} async-done(((f32[64,1,512]{2,1,0:T(1,128)}), f32[64,1,512]{2,1,0:T(1,128)S(1)}, u32[]{:S(2)}, u32[]{:S(2)}) %all-to-all-start) | async-done | bytes 131104 | tf_op jit(solution)/shard_map/all_to_all | solution.py:92
  53.7 2.4 copy.27
  56.1 2.8 all_to_all.16
  59.3 2.5 collective-permute-start.2
  63.1 2.9 collective-permute-start
  66.1 2.9 collective-permute-start.1
  70.1 4.1 collective-permute-done
  74.2 7.7 %collective-permute-done.1 = f32[8,8,8,1]{3,1,2,0:T(8,128)S(1)} collective-permute-done((f32[8,8,8,1]{3,1,2,0:T(8,128)S(1)}, f32[8,8,8,1]{3,1,2,0:T(8,128)S(1)}, u32[]{:S(2)}, u32[]{:S(2)}) %collective-permute-start.1) | collective-permute-done | bytes 2080 | tf_op jit(solution)/shard_map/ppermute | solution.py:17
  82.7 1.3 collective-permute-start.6
  85.5 5.5 %collective-permute-start.4 = (f32[8,8,8,1]{3,1,2,0:T(8,128)S(1)}, f32[8,8,8,1]{3,1,2,0:T(8,128)S(1)}, u32[]{:S(2)}, u32[]{:S(2)}) collective-permute-start(f32[8,8,8,1]{3,1,2,0:T(8,128)S(1)} %get-tuple-element.19), channel_id=1, source_target_pairs={{0,128},{128,256},{256,384},{384,0},{1,129},{129,257},{257,385},{3... | collective-permute-start | bytes 6152 | tf_op jit(solution)/shard_map/ppermute | solution.py:16
  91.0 1.9 collective-permute-start.5
  93.0 7.6 %collective-permute-done.4 = f32[8,8,8,1]{3,1,2,0:T(8,128)S(1)} collective-permute-done((f32[8,8,8,1]{3,1,2,0:T(8,128)S(1)}, f32[8,8,8,1]{3,1,2,0:T(8,128)S(1)}, u32[]{:S(2)}, u32[]{:S(2)}) %collective-permute-start.4) | collective-permute-done | bytes 2080 | tf_op jit(solution)/shard_map/ppermute | solution.py:16
  101.3 2.5 fusion.12
  103.8 2.6 psum.28
  106.5 1.7 fusion
  110.1 4.9 %collective-permute-start.11 = (f32[8,8,1,512]{3,1,2,0:T(8,128)S(1)}, f32[8,8,1,512]{3,1,2,0:T(8,128)S(1)}, u32[]{:S(2)}, u32[]{:S(2)}) collective-permute-start(f32[8,8,1,512]{3,1,2,0:T(8,128)S(1)} %slice.166), channel_id=1, source_target_pairs={{0,2},{2,4},{4,6},{6,8},{8,10},{10,12},{12,14},{14,16},{16,18},{18... | collective-permute-start | bytes 393224 | tf_op jit(solution)/shard_map/ppermute | solution.py:30
  115.2 3.2 collective-permute-start.8
  118.4 3.1 collective-permute-start.9
  122.2 3.8 collective-permute-done.8
  126.0 6.6 %collective-permute-done.9 = f32[8,8,8,1]{3,1,2,0:T(8,128)S(1)} collective-permute-done((f32[8,8,8,1]{3,1,2,0:T(8,128)S(1)}, f32[8,8,8,1]{3,1,2,0:T(8,128)S(1)}, u32[]{:S(2)}, u32[]{:S(2)}) %collective-permute-start.9) | collective-permute-done | bytes 2080 | tf_op jit(solution)/shard_map/ppermute | solution.py:24
  133.6 4.2 collective-permute-start.12
  138.6 5.9 %collective-permute-start.15 = (f32[8,8,1,512]{3,1,2,0:T(8,128)S(1)}, f32[8,8,1,512]{3,1,2,0:T(8,128)S(1)}, u32[]{:S(2)}, u32[]{:S(2)}) collective-permute-start(f32[8,8,1,512]{3,1,2,0:T(8,128)S(1)} %slice.174), channel_id=1, source_target_pairs={{0,2},{2,4},{4,6},{6,8},{8,10},{10,12},{12,14},{14,16},{16,18},{18... | collective-permute-start | bytes 393224 | tf_op jit(solution)/shard_map/ppermute | solution.py:30
  146.0 3.7 collective-permute-start.13
  149.8 7.5 %collective-permute-done.13 = f32[8,8,8,1]{3,1,2,0:T(8,128)S(1)} collective-permute-done((f32[8,8,8,1]{3,1,2,0:T(8,128)S(1)}, f32[8,8,8,1]{3,1,2,0:T(8,128)S(1)}, u32[]{:S(2)}, u32[]{:S(2)}) %collective-permute-start.13) | collective-permute-done | bytes 2080 | tf_op jit(solution)/shard_map/ppermute | solution.py:24
  157.8 9.1 %collective-permute-done.14 = f32[8,8,1,512]{3,1,2,0:T(8,128)S(1)} collective-permute-done((f32[8,8,1,512]{3,1,2,0:T(8,128)S(1)}, f32[8,8,1,512]{3,1,2,0:T(8,128)S(1)}, u32[]{:S(2)}, u32[]{:S(2)}) %collective-permute-start.14) | collective-permute-done | bytes 131104 | tf_op jit(solution)/shard_map/ppermute | solution.py:30
  168.8 66.4 %all-reduce.2.cloned.1.call-done = f32[8,8,512]{2,1,0:T(8,128)} async-done(((f32[8,8,512]{2,1,0:T(8,128)}), f32[8,8,512]{2,1,0:T(8,128)}) %all-reduce.2.cloned.1.call-update) | async-done | bytes 131088 | tf_op jit(solution)/shard_map/psum | solution.py:123
  235.3 1.7 multiply_reduce_fusion.1
  237.0 9.7 %psum.30 = f32[8]{0:T(128)S(1)} all-reduce(f32[8]{0:T(128)S(1)} %get-tuple-element.33), channel_id=1, replica_groups=mesh['face'=4,'tile'=64,'lev'=2] {'face'}, use_global_device_ids=true, to_apply=%region_6.7 | all-reduce | flops 8 | bytes 64 | tf_op jit(solution)/shard_map/psum | solution.py:125
  246.7 224.8 %psum.31 = f32[8]{0:T(128)S(1)} all-reduce(f32[8]{0:T(128)S(1)} %psum.30), channel_id=1, replica_groups=mesh['face'=4,'tile'=64,'lev'=2] {'tile'}, use_global_device_ids=true, to_apply=%region_7.8 | all-reduce | flops 8 | bytes 64 | tf_op jit(solution)/shard_map/psum | solution.py:125
  (79 shorter events, 16.8 us)
Async XLA Ops:
  7.2 23.8 %copy-start = (f32[2,8,8,512]{3,2,1,0:T(8,128)S(1)}, f32[2,8,8,512]{3,2,1,0:T(8,128)}, u32[]{:S(2)}) copy-start(f32[2,8,8,512]{3,2,1,0:T(8,128)} %param.13) | copy-start | bytes 786436
  7.2 23.8 %copy-start.1 = (s32[2,8,8,512]{3,2,1,0:T(8,128)S(1)}, s32[2,8,8,512]{3,2,1,0:T(8,128)}, u32[]{:S(2)}) copy-start(s32[2,8,8,512]{3,2,1,0:T(8,128)} %param.14) | copy-start | bytes 786436
  10.6 40.5 %all-to-all-start = ((f32[64,1,512]{2,1,0:T(1,128)}), f32[64,1,512]{2,1,0:T(1,128)S(1)}, u32[]{:S(2)}, u32[]{:S(2)}) async-start(f32[64,1,512]{2,1,0:T(1,128)} %reshape.69), calls=%async_computation | async-start | bytes 262144 | tf_op jit(solution)/shard_map/all_to_all | solution.py:92
  30.9 204.3 %all-reduce.2.cloned.1.call-start = ((), (), s32[]{:S(2)}) async-start(), calls=%async_computation.1 | async-start | bytes 262144 | tf_op jit(solution)/shard_map/psum | solution.py:123
  56.1 2.8 copy-start.4
  59.3 22.6 %collective-permute-start.2 = (f32[8,8,1,512]{3,1,2,0:T(8,128)S(1)}, f32[8,8,1,512]{3,1,2,0:T(8,128)S(1)}, u32[]{:S(2)}, u32[]{:S(2)}) collective-permute-start(f32[8,8,1,512]{3,1,2,0:T(8,128)S(1)} %get-tuple-element.25), channel_id=1, source_target_pairs={{0,2},{2,4},{4,6},{6,8},{8,10},{10,12},{12,14},{14,16},{16,18},{18... | collective-permute-start | bytes 393224 | tf_op jit(solution)/shard_map/ppermute | solution.py:16
  61.8 20.1 %collective-permute-start.3 = (f32[8,8,1,512]{3,1,2,0:T(8,128)S(1)}, f32[8,8,1,512]{3,1,2,0:T(8,128)S(1)}, u32[]{:S(2)}, u32[]{:S(2)}) collective-permute-start(f32[8,8,1,512]{3,1,2,0:T(8,128)S(1)} %get-tuple-element.26), channel_id=1, source_target_pairs={{2,0},{4,2},{6,4},{8,6},{10,8},{12,10},{14,12},{16,14},{18,16},{20... | collective-permute-start | bytes 393224 | tf_op jit(solution)/shard_map/ppermute | solution.py:17
  63.1 11.1 %collective-permute-start = (f32[8,8,8,1]{3,1,2,0:T(8,128)S(1)}, f32[8,8,8,1]{3,1,2,0:T(8,128)S(1)}, u32[]{:S(2)}, u32[]{:S(2)}) collective-permute-start(f32[8,8,8,1]{3,1,2,0:T(8,128)S(1)} %get-tuple-element.23), channel_id=1, source_target_pairs={{0,128},{128,256},{256,384},{384,0},{1,129},{129,257},{257,385},{3... | collective-permute-start | bytes 6152 | tf_op jit(solution)/shard_map/ppermute | solution.py:16
  66.1 15.9 %collective-permute-start.1 = (f32[8,8,8,1]{3,1,2,0:T(8,128)S(1)}, f32[8,8,8,1]{3,1,2,0:T(8,128)S(1)}, u32[]{:S(2)}, u32[]{:S(2)}) collective-permute-start(f32[8,8,8,1]{3,1,2,0:T(8,128)S(1)} %get-tuple-element.24), channel_id=1, source_target_pairs={{128,0},{256,128},{384,256},{0,384},{129,1},{257,129},{385,257},{1... | collective-permute-start | bytes 6152 | tf_op jit(solution)/shard_map/ppermute | solution.py:17
  82.7 17.8 %collective-permute-start.6 = (f32[8,8,1,512]{3,1,2,0:T(8,128)S(1)}, f32[8,8,1,512]{3,1,2,0:T(8,128)S(1)}, u32[]{:S(2)}, u32[]{:S(2)}) collective-permute-start(f32[8,8,1,512]{3,1,2,0:T(8,128)S(1)} %get-tuple-element.21), channel_id=1, source_target_pairs={{0,2},{2,4},{4,6},{6,8},{8,10},{10,12},{12,14},{14,16},{16,18},{18... | collective-permute-start | bytes 393224 | tf_op jit(solution)/shard_map/ppermute | solution.py:16
  84.0 17.3 %copy-start.2 = (f32[8,1,1,128]{3,2,1,0:T(1,128)S(1)}, f32[8,1,1,128]{3,2,1,0:T(1,128)}, u32[]{:S(2)}) copy-start(f32[8,1,1,128]{3,2,1,0:T(1,128)} %param.18) | copy-start | bytes 12292
  84.0 17.3 %copy-start.8 = (s32[1,1,128]{2,1,0:T(1,128)S(1)}, s32[1,1,128]{2,1,0:T(1,128)}, u32[]{:S(2)}) copy-start(s32[1,1,128]{2,1,0:T(1,128)} %param.15) | copy-start | bytes 1540
  84.0 16.5 %collective-permute-start.7 = (f32[8,8,1,512]{3,1,2,0:T(8,128)S(1)}, f32[8,8,1,512]{3,1,2,0:T(8,128)S(1)}, u32[]{:S(2)}, u32[]{:S(2)}) collective-permute-start(f32[8,8,1,512]{3,1,2,0:T(8,128)S(1)} %get-tuple-element.22), channel_id=1, source_target_pairs={{2,0},{4,2},{6,4},{8,6},{10,8},{12,10},{14,12},{16,14},{18,16},{20... | collective-permute-start | bytes 393224 | tf_op jit(solution)/shard_map/ppermute | solution.py:17
  85.5 15.0 %collective-permute-start.4 = (f32[8,8,8,1]{3,1,2,0:T(8,128)S(1)}, f32[8,8,8,1]{3,1,2,0:T(8,128)S(1)}, u32[]{:S(2)}, u32[]{:S(2)}) collective-permute-start(f32[8,8,8,1]{3,1,2,0:T(8,128)S(1)} %get-tuple-element.19), channel_id=1, source_target_pairs={{0,128},{128,256},{256,384},{384,0},{1,129},{129,257},{257,385},{3... | collective-permute-start | bytes 6152 | tf_op jit(solution)/shard_map/ppermute | solution.py:16
  91.0 9.6 %collective-permute-start.5 = (f32[8,8,8,1]{3,1,2,0:T(8,128)S(1)}, f32[8,8,8,1]{3,1,2,0:T(8,128)S(1)}, u32[]{:S(2)}, u32[]{:S(2)}) collective-permute-start(f32[8,8,8,1]{3,1,2,0:T(8,128)S(1)} %get-tuple-element.20), channel_id=1, source_target_pairs={{128,0},{256,128},{384,256},{0,384},{129,1},{257,129},{385,257},{1... | collective-permute-start | bytes 6152 | tf_op jit(solution)/shard_map/ppermute | solution.py:17
  92.9 10.9 %copy-start.3 = (f32[8,1,1,128]{3,2,1,0:T(1,128)S(1)}, f32[8,1,1,128]{3,2,1,0:T(1,128)}, u32[]{:S(2)}) copy-start(f32[8,1,1,128]{3,2,1,0:T(1,128)} %param.17) | copy-start | bytes 12292
  92.9 13.5 %copy-start.6 = (f32[1,1,128]{2,1,0:T(1,128)S(1)}, f32[1,1,128]{2,1,0:T(1,128)}, u32[]{:S(2)}) copy-start(f32[1,1,128]{2,1,0:T(1,128)} %param.19) | copy-start | bytes 1540
  92.9 13.5 %copy-start.7 = (f32[1,1,128]{2,1,0:T(1,128)S(1)}, f32[1,1,128]{2,1,0:T(1,128)}, u32[]{:S(2)}) copy-start(f32[1,1,128]{2,1,0:T(1,128)} %param.20) | copy-start | bytes 1540
  108.8 23.7 %collective-permute-start.10 = (f32[8,8,1,512]{3,1,2,0:T(8,128)S(1)}, f32[8,8,1,512]{3,1,2,0:T(8,128)S(1)}, u32[]{:S(2)}, u32[]{:S(2)}) collective-permute-start(f32[8,8,1,512]{3,1,2,0:T(8,128)S(1)} %slice.165), channel_id=1, source_target_pairs={{2,0},{4,2},{6,4},{8,6},{10,8},{12,10},{14,12},{16,14},{18,16},{20... | collective-permute-start | bytes 393224 | tf_op jit(solution)/shard_map/ppermute | solution.py:30
  110.1 22.4 %collective-permute-start.11 = (f32[8,8,1,512]{3,1,2,0:T(8,128)S(1)}, f32[8,8,1,512]{3,1,2,0:T(8,128)S(1)}, u32[]{:S(2)}, u32[]{:S(2)}) collective-permute-start(f32[8,8,1,512]{3,1,2,0:T(8,128)S(1)} %slice.166), channel_id=1, source_target_pairs={{0,2},{2,4},{4,6},{6,8},{8,10},{10,12},{12,14},{14,16},{16,18},{18... | collective-permute-start | bytes 393224 | tf_op jit(solution)/shard_map/ppermute | solution.py:30
  115.2 10.7 %collective-permute-start.8 = (f32[8,8,8,1]{3,1,2,0:T(8,128)S(1)}, f32[8,8,8,1]{3,1,2,0:T(8,128)S(1)}, u32[]{:S(2)}, u32[]{:S(2)}) collective-permute-start(f32[8,8,8,1]{3,1,2,0:T(8,128)S(1)} %slice.161), channel_id=1, source_target_pairs={{0,384},{128,0},{256,128},{384,256},{1,385},{129,1},{257,129},{385... | collective-permute-start | bytes 6152 | tf_op jit(solution)/shard_map/ppermute | solution.py:24
  118.4 14.1 %collective-permute-start.9 = (f32[8,8,8,1]{3,1,2,0:T(8,128)S(1)}, f32[8,8,8,1]{3,1,2,0:T(8,128)S(1)}, u32[]{:S(2)}, u32[]{:S(2)}) collective-permute-start(f32[8,8,8,1]{3,1,2,0:T(8,128)S(1)} %slice.162), channel_id=1, source_target_pairs={{0,128},{128,256},{256,384},{384,0},{1,129},{129,257},{257,385},{3... | collective-permute-start | bytes 6152 | tf_op jit(solution)/shard_map/ppermute | solution.py:24
  133.6 16.0 %collective-permute-start.12 = (f32[8,8,8,1]{3,1,2,0:T(8,128)S(1)}, f32[8,8,8,1]{3,1,2,0:T(8,128)S(1)}, u32[]{:S(2)}, u32[]{:S(2)}) collective-permute-start(f32[8,8,8,1]{3,1,2,0:T(8,128)S(1)} %slice.169), channel_id=1, source_target_pairs={{0,384},{128,0},{256,128},{384,256},{1,385},{129,1},{257,129},{385... | collective-permute-start | bytes 6152 | tf_op jit(solution)/shard_map/ppermute | solution.py:24
  138.6 19.1 %collective-permute-start.15 = (f32[8,8,1,512]{3,1,2,0:T(8,128)S(1)}, f32[8,8,1,512]{3,1,2,0:T(8,128)S(1)}, u32[]{:S(2)}, u32[]{:S(2)}) collective-permute-start(f32[8,8,1,512]{3,1,2,0:T(8,128)S(1)} %slice.174), channel_id=1, source_target_pairs={{0,2},{2,4},{4,6},{6,8},{8,10},{10,12},{12,14},{14,16},{16,18},{18... | collective-permute-start | bytes 393224 | tf_op jit(solution)/shard_map/ppermute | solution.py:30
  144.5 22.3 %collective-permute-start.14 = (f32[8,8,1,512]{3,1,2,0:T(8,128)S(1)}, f32[8,8,1,512]{3,1,2,0:T(8,128)S(1)}, u32[]{:S(2)}, u32[]{:S(2)}) collective-permute-start(f32[8,8,1,512]{3,1,2,0:T(8,128)S(1)} %slice.173), channel_id=1, source_target_pairs={{2,0},{4,2},{6,4},{8,6},{10,8},{12,10},{14,12},{16,14},{18,16},{20... | collective-permute-start | bytes 393224 | tf_op jit(solution)/shard_map/ppermute | solution.py:30
  146.0 11.4 %collective-permute-start.13 = (f32[8,8,8,1]{3,1,2,0:T(8,128)S(1)}, f32[8,8,8,1]{3,1,2,0:T(8,128)S(1)}, u32[]{:S(2)}, u32[]{:S(2)}) collective-permute-start(f32[8,8,8,1]{3,1,2,0:T(8,128)S(1)} %slice.170), channel_id=1, source_target_pairs={{0,128},{128,256},{256,384},{384,0},{1,129},{129,257},{257,385},{3... | collective-permute-start | bytes 6152 | tf_op jit(solution)/shard_map/ppermute | solution.py:24
  166.9 68.3 %copy-start.5 = (f32[8]{0:T(128)S(1)}, f32[8]{0:T(128)}, u32[]{:S(2)}) copy-start(f32[8]{0:T(128)} %param.21) | copy-start | bytes 100
Sparse Core Ops, SparseCore 0:
  169.0 66.2 all-reduce.1
